TPU v7x, 32 devices: a whole 2x2x4 slice. The times are simulated.
32 devices in a mesh: ctx: 8 (over z, y), chan: 4 (over x, core).
Axes of the slice: x: 2, y: 2, z: 4, core: 2. Of those that a mesh axis runs over, the one named last changes fastest.
Arguments:
- layer_in: float32 [1024, 8192], P('ctx', 'chan'), may hold values from -64 to 64
- query_mr: float32 [1024, 8192], P('ctx', 'chan'), may hold values from -6 to 6
- key_mr: float32 [1024, 8192], P('ctx', 'chan'), may hold values from -6 to 6
- query_lr: float32 [1024, 8192], P('ctx', 'chan'), may hold values from -6 to 6
- key_lr: float32 [1024, 8192], P('ctx', 'chan'), may hold values from -6 to 6
- filter_mr: float32 [128, 8192], P(None, 'chan'), may hold values from -0.5 to 0.5
- filter_lr: float32 [1024, 8192], P('ctx', 'chan'), may hold values from -0.1875 to 0.1875
- norm_gain: float32 [8192], P('chan'), may hold values from 0.1 to 1.9
- out_grad: float32 [1024, 8192], P('ctx', 'chan'), may hold values from -6 to 6
Outputs:
- grad_in: float32 [1024, 8192], P('ctx', 'chan')
- grad_query_mr: float32 [1024, 8192], P('ctx', 'chan')
- grad_key_mr: float32 [1024, 8192], P('ctx', 'chan')
- grad_filter_mr: float32 [128, 8192], P(None, 'chan')
- grad_gain: float32 [8192], P('chan')
- grad_query_lr: float32 [1024, 8192], P('ctx', 'chan')
- grad_key_lr: float32 [1024, 8192], P('ctx', 'chan')
- grad_filter_lr: float32 [1024, 8192], P('ctx', 'chan')
All inputs are finite; a program needn't handle non-finite values.
Results may differ from a plain program's by a relative error of at most 0.0003.
Values sent between devices are 32-bit elements; how exact they have to be, the bound alone decides.
A program may use at most 128 MiB of HBM per device.

v0:
```python
import math

import jax
import jax.numpy as jnp
import numpy as np
from jax import lax
from jax.experimental.layout import Layout, with_layout_constraint
from jax.sharding import PartitionSpec as P


def shifted(shard, axis, by):
    peers = lax.axis_size(axis)
    pairs = [(i, i + by) for i in range(peers) if 0 <= i + by < peers]
    return lax.ppermute(shard, axis, pairs)


def mult_in(form, left, right):
    return jnp.einsum(form, left, right, precision=lax.Precision.HIGHEST)


def dft_tables(half_rows):
    freq_rows = 2 * half_rows
    grid_total = freq_rows * 128
    first_freq = jnp.arange(freq_rows, dtype=jnp.int32)
    first_half = jnp.arange(half_rows, dtype=jnp.int32)
    second_idx = jnp.arange(128, dtype=jnp.int32)
    angle_one = (first_freq[:, None] * first_half[None, :] % freq_rows).astype(jnp.float32) * (
        2.0 * math.pi / freq_rows
    )
    angle_turn = (first_freq[:, None] * second_idx[None, :] % grid_total).astype(jnp.float32) * (
        2.0 * math.pi / grid_total
    )
    angle_two = (second_idx[:, None] * second_idx[None, :] % 128).astype(jnp.float32) * (
        2.0 * math.pi / 128
    )
    return (
        jnp.cos(angle_one),
        -jnp.sin(angle_one),
        jnp.cos(angle_turn),
        -jnp.sin(angle_turn),
        jnp.cos(angle_two),
        -jnp.sin(angle_two),
    )


def forward_dft(signal, tables):
    cos_one, sin_one, cos_turn, sin_turn, cos_two, sin_two = tables
    first_re = mult_in("kn,cnm->ckm", cos_one, signal)
    first_im = mult_in("kn,cnm->ckm", sin_one, signal)
    turned_re = first_re * cos_turn - first_im * sin_turn
    turned_im = first_re * sin_turn + first_im * cos_turn
    spec_re = mult_in("ckm,jm->ckj", turned_re, cos_two) - mult_in(
        "ckm,jm->ckj", turned_im, sin_two
    )
    spec_im = mult_in("ckm,jm->ckj", turned_re, sin_two) + mult_in(
        "ckm,jm->ckj", turned_im, cos_two
    )
    return (spec_re, spec_im)


def inverse_dft(spec_re, spec_im, tables):
    cos_one, sin_one, cos_turn, sin_turn, cos_two, sin_two = tables
    grid_total = cos_turn.shape[0] * 128
    first_re = mult_in("ckj,jm->ckm", spec_re, cos_two) + mult_in("ckj,jm->ckm", spec_im, sin_two)
    first_im = mult_in("ckj,jm->ckm", spec_im, cos_two) - mult_in("ckj,jm->ckm", spec_re, sin_two)
    turned_re = first_re * cos_turn + first_im * sin_turn
    turned_im = first_im * cos_turn - first_re * sin_turn
    signal = mult_in("kn,ckm->cnm", cos_one, turned_re) + mult_in("kn,ckm->cnm", sin_one, turned_im)
    return signal * (1.0 / grid_total)


def long_pass(pieces):
    values, grad_pieces, filt_piece = pieces
    item_count = values.shape[1]
    length = values.shape[2]
    half_rows = length // 128
    tables = dft_tables(half_rows)

    def shaped(array):
        return array.reshape(item_count, half_rows, 128)

    def flat(array):
        return array.reshape(1, item_count, length)

    vals_re, vals_im = forward_dft(shaped(values), tables)
    grads_re, grads_im = forward_dft(shaped(grad_pieces), tables)
    filt_re, filt_im = forward_dft(shaped(filt_piece), tables)
    conv_full = inverse_dft(
        vals_re * filt_re - vals_im * filt_im, vals_re * filt_im + vals_im * filt_re, tables
    )
    back_full = inverse_dft(
        filt_re * grads_re + filt_im * grads_im, filt_re * grads_im - filt_im * grads_re, tables
    )
    filter_full = inverse_dft(
        vals_re * grads_re + vals_im * grads_im, vals_re * grads_im - vals_im * grads_re, tables
    )
    return (
        lax.all_to_all(flat(conv_full), "ctx", split_axis=2, concat_axis=0, tiled=True),
        lax.all_to_all(flat(back_full), "ctx", split_axis=2, concat_axis=0, tiled=True),
        lax.all_to_all(flat(filter_full), "ctx", split_axis=2, concat_axis=0, tiled=True),
    )


def to_channel_rows(array, group_count):
    return array.T.reshape(group_count, array.shape[1] // group_count, array.shape[0])


def back_to_tokens(array):
    return array.reshape(array.shape[0] * array.shape[1], array.shape[2]).T


DENSE_TABLE_BYTES = 16 * 2**20


def half_step_table(period, rows):
    halves = period // 2
    steps = (2 * np.arange(halves)[:, None] + 1) * np.arange(rows)[None, :] % (2 * period)
    angle = steps * (math.pi / period)
    return np.concatenate([np.cos(angle), -np.sin(angle)], 0).astype(np.float32)


def to_spec(table, signal):
    return jnp.dot(table, signal, precision=lax.Precision.HIGH)


def from_spec(table, spec):
    back_table = np.ascontiguousarray(table.T * np.float32(2.0 / table.shape[0]))
    return jnp.dot(back_table, spec, precision=lax.Precision.HIGH)


def times(left, right):
    half = left.shape[0] // 2
    lr, li, rr, ri = left[:half], left[half:], right[:half], right[half:]
    return jnp.concatenate([lr * rr - li * ri, lr * ri + li * rr], 0)


def conj_times(left, right):
    half = left.shape[0] // 2
    lr, li, rr, ri = left[:half], left[half:], right[:half], right[half:]
    return jnp.concatenate([lr * rr + li * ri, lr * ri - li * rr], 0)


def rows_first(array):
    return with_layout_constraint(array, Layout(major_to_minor=tuple(range(array.ndim))))


def by_groups(array):
    groups = lax.axis_size("ctx")
    width = array.shape[1] // groups
    array = rows_first(array)
    return jnp.stack([array[:, i * width : (i + 1) * width] for i in range(groups)])


def gather_tokens(array):
    pieces = rows_first(by_groups(array))
    pieces = rows_first(lax.all_to_all(pieces, "ctx", split_axis=0, concat_axis=0))
    return pieces.reshape(-1, pieces.shape[2])


def scatter_tokens(array):
    groups = lax.axis_size("ctx")
    pieces = rows_first(rows_first(array).reshape(groups, -1, array.shape[1]))
    pieces = rows_first(lax.all_to_all(pieces, "ctx", split_axis=0, concat_axis=0))
    return rows_first(jnp.concatenate([pieces[i] for i in range(groups)], 1))


def after(array, *earlier):
    return lax.optimization_barrier((array, *earlier))[0]


def both_tokens(first, second):
    pieces = rows_first(jnp.concatenate([by_groups(first), by_groups(second)], 1))
    pieces = rows_first(lax.all_to_all(pieces, "ctx", split_axis=0, concat_axis=0))
    half = first.shape[0]
    return (
        pieces[:, :half].reshape(-1, pieces.shape[2]),
        pieces[:, half:].reshape(-1, pieces.shape[2]),
    )


def split_long_pass(long_in, grad_conv_lr, filter_lr):
    group_count = lax.axis_size("ctx")
    results = long_pass(
        tuple(
            lax.all_to_all(
                to_channel_rows(array, group_count), "ctx", split_axis=0, concat_axis=2, tiled=True
            )
            for array in (long_in, grad_conv_lr, filter_lr)
        )
    )
    return tuple(back_to_tokens(result) for result in results)


def shards(layer_in, query_mr, key_mr, query_lr, key_lr, filter_mr, filter_lr, norm_gain, out_grad):
    row_count, chan_count = layer_in.shape
    tap_count = filter_mr.shape[0]
    full_width = chan_count * lax.axis_size("chan")
    length = row_count * lax.axis_size("ctx")
    medium = half_step_table(row_count + tap_count, row_count + tap_count)
    own_table, next_table = medium[:, :row_count], medium[:, row_count:]
    tap_table = medium[:, :tap_count]
    grad_conv_lr = out_grad * query_lr
    mixed_in = key_mr * layer_in
    preceding = shifted(mixed_in[row_count - tap_count :], "ctx", 1)
    filt_spec = to_spec(tap_table, filter_mr)
    mixed_spec = to_spec(own_table, mixed_in) - to_spec(next_table, preceding)
    conv_mr = from_spec(own_table, times(mixed_spec, filt_spec))
    dense = 8 * length * length <= DENSE_TABLE_BYTES
    if dense:
        table = half_step_table(2 * length, length)
        filt_all, grad_all = both_tokens(filter_lr, grad_conv_lr)
    residual = layer_in + query_mr * conv_mr
    square_sum = lax.psum(jnp.sum(residual * residual, axis=1), "chan")
    inv_rms = lax.rsqrt(square_sum / full_width + 1e-06)[:, None]
    normed = residual * inv_rms * norm_gain
    long_in = key_lr * normed
    if dense:
        val_all = gather_tokens(after(long_in, filt_all))
        long_filt = to_spec(table, filt_all)
        long_grad = to_spec(table, grad_all)
        back_all = from_spec(table, conj_times(long_filt, long_grad))
        grad_long_in = scatter_tokens(after(back_all, val_all))
        long_val = to_spec(table, val_all)
        conv_all = from_spec(table, times(long_val, long_filt))
        conv_lr = scatter_tokens(after(conv_all, grad_long_in))
    else:
        conv_lr, grad_long_in, grad_filter_lr = split_long_pass(long_in, grad_conv_lr, filter_lr)
    grad_query_lr = out_grad * conv_lr
    grad_key_lr = grad_long_in * normed
    grad_normed = grad_long_in * key_lr
    gain_part = jnp.sum(grad_normed * residual * inv_rms, axis=0)
    scaled = norm_gain * grad_normed
    cross_sum = lax.psum(jnp.sum(scaled * residual, axis=1), "chan")
    grad_resid = (
        out_grad + inv_rms * scaled - residual * inv_rms**3 * (cross_sum / full_width)[:, None]
    )
    grad_query_mr = grad_resid * conv_mr
    grad_conv_mr = grad_resid * query_mr
    following = shifted(grad_conv_mr[:tap_count], "ctx", -1)
    own_spec = to_spec(own_table, grad_conv_mr)
    filter_part = from_spec(tap_table, conj_times(mixed_spec, own_spec))
    spare = jnp.zeros((-(tap_count + 1) % 8, chan_count), jnp.float32)
    parts = jnp.concatenate([filter_part, gain_part[None], spare], 0)
    parts = gather_tokens(after(parts, conv_lr))
    sums = jnp.sum(parts.reshape(lax.axis_size("ctx"), -1, parts.shape[1]), axis=0)
    if dense:
        filt_all = from_spec(table, conj_times(long_val, long_grad))
        grad_filter_lr = scatter_tokens(after(filt_all, parts))
    sums = lax.all_gather(sums, "ctx", axis=1, tiled=True)
    grad_filter_mr, grad_gain = sums[:tap_count], sums[tap_count]
    grad_spec = own_spec + to_spec(next_table, following)
    grad_mixed = from_spec(own_table, conj_times(filt_spec, grad_spec))
    grad_key_mr = grad_mixed * layer_in
    grad_in = grad_resid + grad_mixed * key_mr
    return (
        grad_in,
        grad_query_mr,
        grad_key_mr,
        grad_filter_mr,
        grad_gain,
        grad_query_lr,
        grad_key_lr,
        grad_filter_lr,
    )


def solution(mesh):
    in_specs = (
        P("ctx", "chan"),
        P("ctx", "chan"),
        P("ctx", "chan"),
        P("ctx", "chan"),
        P("ctx", "chan"),
        P(None, "chan"),
        P("ctx", "chan"),
        P("chan"),
        P("ctx", "chan"),
    )
    out_specs = (
        P("ctx", "chan"),
        P("ctx", "chan"),
        P("ctx", "chan"),
        P(None, "chan"),
        P("chan"),
        P("ctx", "chan"),
        P("ctx", "chan"),
        P("ctx", "chan"),
    )
    return jax.shard_map(shards, mesh=mesh, in_specs=in_specs, out_specs=out_specs, check_vma=False)
```

profile of v0, /device:TPU:0, one launch (start us, length us, event | category | flops | bytes accessed | tf_op | source)
XLA Modules:
  0.0 324.8 jit_solution(10101872643682232432)
XLA Ops:
  7.2 1.8 mul.173
  9.3 1.6 pad_maximum_fusion
  10.9 7.4 %all-to-all-start = ((f32[8,256,256]{2,1,0:T(8,128)}), f32[8,256,256]{2,1,0:T(8,128)}, u32[]{:S(2)}, u32[]{:S(2)}) async-start(f32[8,256,256]{2,1,0:T(8,128)} %pad_maximum_fusion), calls=%async_computation | async-start | bytes 4194304 | tf_op jit(solution)/shard_map/all_to_all | solution.py:173
  18.5 4.0 %collective-permute-start = (f32[128,2048]{1,0:T(8,128)S(1)}, f32[128,2048]{1,0:T(8,128)S(1)}, u32[]{:S(2)}, u32[]{:S(2)}) collective-permute-start(f32[128,2048]{1,0:T(8,128)S(1)} %mul.164), channel_id=1, source_target_pairs={{0,4},{4,8},{8,12},{12,16},{16,20},{20,24},{24,28},{1,5},{5,9},{9,... | collective-permute-start | bytes 3145736 | tf_op jit(solution)/shard_map/ppermute | solution.py:14
  24.6 38.8 %collective-permute-done = f32[128,2048]{1,0:T(8,128)S(1)} collective-permute-done((f32[128,2048]{1,0:T(8,128)S(1)}, f32[128,2048]{1,0:T(8,128)S(1)}, u32[]{:S(2)}, u32[]{:S(2)}) %collective-permute-start) | collective-permute-done | bytes 1048608 | tf_op jit(solution)/shard_map/ppermute | solution.py:14
  66.5 1.9 multiply_reduce_fusion.2
  68.4 5.7 %psum.14 = f32[128]{0:T(128)S(1)} all-reduce(f32[128]{0:T(128)S(1)} %get-tuple-element.20), channel_id=1, replica_groups=mesh['ctx'=8,'chan'=4] {'chan'}, use_global_device_ids=true, to_apply=%region_1.0 | all-reduce | flops 128 | bytes 1024 | tf_op jit(solution)/shard_map/psum | solution.py:213
  75.3 2.7 fusion.132
  83.3 29.5 %all-to-all-start.1 = ((f32[8,128,256]{2,1,0:T(8,128)}), f32[8,128,256]{2,1,0:T(8,128)}, u32[]{:S(2)}, u32[]{:S(2)}) async-start(f32[8,128,256]{2,1,0:T(8,128)} %bitcast_dynamic-update-slice_fusion.8), calls=%async_computation.1 | async-start | bytes 2097152 | tf_op jit(solution)/shard_map/all_to_all | solution.py:156
  112.9 6.0 %fusion.136 = f32[2048,256]{1,0:T(8,128)S(1)} fusion(f32[2048,1024]{1,0:T(8,128)} %constant.22.clone, f32[1024,256]{1,0:T(8,128)S(1)} %bitcast.230), kind=kOutput, calls=%fused_computation.212 | convolution fusion | flops 3221225472 | bytes 11534336 | tf_op jit(solution)/shard_map/dot_general | solution.py:123
  118.9 6.7 %fusion.137 = f32[2048,256]{1,0:T(8,128)S(1)} fusion(f32[2048,1024]{1,0:T(8,128)} %constant.22.clone, f32[1024,256]{1,0:T(8,128)S(1)} %bitcast.229), kind=kOutput, calls=%fused_computation.213 | convolution fusion | flops 3221225472 | bytes 11534336 | tf_op jit(solution)/shard_map/dot_general | solution.py:123
  125.6 2.0 fusion.38
  127.7 3.0 fusion.6
  130.8 7.9 %all-to-all-done.1 = f32[8,128,256]{2,1,0:T(8,128)} async-done(((f32[8,128,256]{2,1,0:T(8,128)}), f32[8,128,256]{2,1,0:T(8,128)}, u32[]{:S(2)}, u32[]{:S(2)}) %all-to-all-start.1) | async-done | bytes 1048608 | tf_op jit(solution)/shard_map/all_to_all | solution.py:156
  138.6 4.5 %all-to-all-start.2 = ((f32[8,128,256]{2,1,0:T(8,128)}), f32[8,128,256]{2,1,0:T(8,128)}, u32[]{:S(2)}, u32[]{:S(2)}) async-start(f32[8,128,256]{2,1,0:T(8,128)} %bitcast.228), calls=%async_computation.2 | async-start | bytes 2097152 | tf_op jit(solution)/shard_map/all_to_all | solution.py:163
  143.1 6.4 %fusion.139 = f32[2048,256]{1,0:T(8,128)S(1)} fusion(f32[2048,1024]{1,0:T(8,128)} %constant.22.clone, f32[1024,256]{1,0:T(8,128)} %bitcast.29), kind=kOutput, calls=%fused_computation.215 | convolution fusion | flops 3221225472 | bytes 11534336 | tf_op jit(solution)/shard_map/dot_general | solution.py:123
  149.5 1.9 fusion.17
  152.5 3.0 fusion.5
  155.4 11.9 %all-to-all-done.2 = f32[8,128,256]{2,1,0:T(8,128)} async-done(((f32[8,128,256]{2,1,0:T(8,128)}), f32[8,128,256]{2,1,0:T(8,128)}, u32[]{:S(2)}, u32[]{:S(2)}) %all-to-all-start.2) | async-done | bytes 1048608 | tf_op jit(solution)/shard_map/all_to_all | solution.py:163
  167.4 1.6 fusion.122
  168.9 1.6 fusion.121
  170.5 1.6 fusion.120
  172.1 1.6 fusion.119
  173.6 1.6 fusion.118
  175.2 1.6 fusion.117
  176.8 1.6 fusion.116
  178.3 1.6 fusion.115
  179.9 4.2 %all-to-all-start.3 = ((f32[8,128,256]{2,1,0:T(8,128)}), f32[8,128,256]{2,1,0:T(8,128)}, u32[]{:S(2)}, u32[]{:S(2)}) async-start(f32[8,128,256]{2,1,0:T(8,128)} %bitcast.227), calls=%async_computation.3 | async-start | bytes 2097152 | tf_op jit(solution)/shard_map/all_to_all | solution.py:163
  184.8 4.9 %fusion.10 = f32[256,1024]{0,1:T(8,128)S(1)} fusion(f32[1024,1024]{1,0:T(8,128)} %constant.26, f32[2048,256]{1,0:T(8,128)} %copy-done.11, f32[2048,256]{1,0:T(8,128)S(1)} %fusion.137), kind=kOutput, calls=%fused_computation.20 | convolution fusion | flops 1611399168 | bytes 9437184 | tf_op jit(solution)/shard_map/dot_general | solution.py:128
  189.7 3.0 fusion.4
  192.7 2.7 multiply_reduce_fusion
  195.5 6.8 %psum.15 = f32[128]{0:T(128)S(1)} all-reduce(f32[128]{0:T(128)S(1)} %get-tuple-element.17), channel_id=1, replica_groups=mesh['ctx'=8,'chan'=4] {'chan'}, use_global_device_ids=true, to_apply=%region_3.0 | all-reduce | flops 128 | bytes 1024 | tf_op jit(solution)/shard_map/psum | solution.py:233
  202.8 7.0 %all-to-all-done.3 = f32[8,128,256]{2,1,0:T(8,128)} async-done(((f32[8,128,256]{2,1,0:T(8,128)}), f32[8,128,256]{2,1,0:T(8,128)}, u32[]{:S(2)}, u32[]{:S(2)}) %all-to-all-start.3) | async-done | bytes 1048608 | tf_op jit(solution)/shard_map/all_to_all | solution.py:163
  209.8 4.6 %all-to-all-start.5 = ((f32[8,128,256]{2,1,0:T(8,128)}), f32[8,128,256]{2,1,0:T(8,128)}, u32[]{:S(2)}, u32[]{:S(2)}) async-start(f32[8,128,256]{2,1,0:T(8,128)} %bitcast.226), calls=%async_computation.5 | async-start | bytes 2097152 | tf_op jit(solution)/shard_map/all_to_all | solution.py:163
  222.0 3.2 fusion.131
  234.1 5.4 %all-to-all-done.5 = f32[8,128,256]{2,1,0:T(8,128)} async-done(((f32[8,128,256]{2,1,0:T(8,128)}), f32[8,128,256]{2,1,0:T(8,128)}, u32[]{:S(2)}, u32[]{:S(2)}) %all-to-all-start.5) | async-done | bytes 1048608 | tf_op jit(solution)/shard_map/all_to_all | solution.py:163
  239.6 4.3 %all-to-all-start.4 = ((f32[8,136,256]{2,1,0:T(8,128)}), f32[8,136,256]{2,1,0:T(8,128)}, u32[]{:S(2)}, u32[]{:S(2)}) async-start(f32[8,136,256]{2,1,0:T(8,128)} %bitcast_dynamic-update-slice_fusion), calls=%async_computation.4 | async-start | bytes 2228224 | tf_op jit(solution)/shard_map/all_to_all | solution.py:156
  243.9 1.6 fusion.106
  245.5 1.6 fusion.105
  249.9 1.6 fusion.103
  251.5 21.0 %all-to-all-done.4 = f32[8,136,256]{2,1,0:T(8,128)} async-done(((f32[8,136,256]{2,1,0:T(8,128)}), f32[8,136,256]{2,1,0:T(8,128)}, u32[]{:S(2)}, u32[]{:S(2)}) %all-to-all-start.4) | async-done | bytes 1114144 | tf_op jit(solution)/shard_map/all_to_all | solution.py:156
  272.5 2.0 reduce_sum.39
  274.5 1.6 fusion.102
  279.2 1.6 fusion.99
  280.8 2.4 convolution_add_fusion
  285.1 2.2 fusion.133
  287.3 26.9 %all-gather.2.cloned.1.call-done = f32[136,2048]{1,0:T(8,128)} async-done(((f32[136,256]{1,0:T(8,128)}), f32[136,2048]{1,0:T(8,128)}) %all-gather.2.cloned.1.call-update) | async-done | bytes 1114128 | tf_op jit(solution)/shard_map/all_gather | solution.py:249
  314.2 2.3 slice.358
  (146 shorter events, 40.0 us)
Async XLA Ops:
  7.2 16.4 %copy-start = (f32[128,2048]{1,0:T(8,128)S(1)}, f32[128,2048]{1,0:T(8,128)}, u32[]{:S(2)}) copy-start(f32[128,2048]{1,0:T(8,128)} %param.24) | copy-start | bytes 3145732
  7.2 2.0 copy-start.30
  10.9 7.4 %copy-start.20 = (f32[128,2048]{1,0:T(8,128)S(1)}, f32[128,2048]{1,0:T(8,128)}, u32[]{:S(2)}) copy-start(f32[128,2048]{1,0:T(8,128)} %param.19) | copy-start | bytes 3145732
  10.9 7.4 %copy-start.25 = (f32[128,2048]{1,0:T(8,128)S(1)}, f32[128,2048]{1,0:T(8,128)}, u32[]{:S(2)}) copy-start(f32[128,2048]{1,0:T(8,128)} %param.21) | copy-start | bytes 3145732
  10.9 64.4 %all-to-all-start = ((f32[8,256,256]{2,1,0:T(8,128)}), f32[8,256,256]{2,1,0:T(8,128)}, u32[]{:S(2)}, u32[]{:S(2)}) async-start(f32[8,256,256]{2,1,0:T(8,128)} %pad_maximum_fusion), calls=%async_computation | async-start | bytes 4194304 | tf_op jit(solution)/shard_map/all_to_all | solution.py:173
  18.3 4.1 %copy-start.29 = (f32[256,128]{1,0:T(8,128)S(1)}, f32[256,128]{1,0:T(8,128)}, u32[]{:S(2)}) copy-start(f32[256,128]{1,0:T(8,128)} %constant.19.clone) | copy-start | bytes 393220
  18.5 44.9 %collective-permute-start = (f32[128,2048]{1,0:T(8,128)S(1)}, f32[128,2048]{1,0:T(8,128)S(1)}, u32[]{:S(2)}, u32[]{:S(2)}) collective-permute-start(f32[128,2048]{1,0:T(8,128)S(1)} %mul.164), channel_id=1, source_target_pairs={{0,4},{4,8},{8,12},{12,16},{16,20},{20,24},{24,28},{1,5},{5,9},{9,... | collective-permute-start | bytes 3145736 | tf_op jit(solution)/shard_map/ppermute | solution.py:14
  23.5 39.9 %copy-start.33 = (f32[256,128]{1,0:T(8,128)S(1)}, f32[256,128]{1,0:T(8,128)}, u32[]{:S(2)}) copy-start(f32[256,128]{1,0:T(8,128)} %constant.20.clone) | copy-start | bytes 393220
  24.6 40.6 %copy-start.7 = (f32[256,2048]{0,1:T(8,128)}, f32[256,2048]{0,1:T(8,128)S(1)}, u32[]{:S(2)}) copy-start(f32[256,2048]{0,1:T(8,128)S(1)} %fusion.135) | copy-start | bytes 6291460
  24.6 39.9 %copy-start.32 = (f32[128,128]{1,0:T(8,128)S(1)}, f32[128,128]{1,0:T(8,128)}, u32[]{:S(2)}) copy-start(f32[128,128]{1,0:T(8,128)} %constant.24) | copy-start | bytes 196612
  64.5 3.9 %copy-start.9 = (f32[256,2048]{0,1:T(8,128)}, f32[256,2048]{0,1:T(8,128)S(1)}, u32[]{:S(2)}) copy-start(f32[256,2048]{0,1:T(8,128)S(1)} %fusion) | copy-start | bytes 6291460
  64.5 2.0 copy-start.23
  64.5 2.0 copy-start.31
  66.5 8.6 %copy-start.15 = (f32[128,2048]{1,0:T(8,128)S(1)}, f32[128,2048]{1,0:T(8,128)}, u32[]{:S(2)}) copy-start(f32[128,2048]{1,0:T(8,128)} %param.23) | copy-start | bytes 3145732
  66.5 8.6 %copy-start.34 = (f32[2048]{0:T(1024)S(1)}, f32[2048]{0:T(1024)}, u32[]{:S(2)}) copy-start(f32[2048]{0:T(1024)} %param.26) | copy-start | bytes 24580
  83.3 55.3 %all-to-all-start.1 = ((f32[8,128,256]{2,1,0:T(8,128)}), f32[8,128,256]{2,1,0:T(8,128)}, u32[]{:S(2)}, u32[]{:S(2)}) async-start(f32[8,128,256]{2,1,0:T(8,128)} %bitcast_dynamic-update-slice_fusion.8), calls=%async_computation.1 | async-start | bytes 2097152 | tf_op jit(solution)/shard_map/all_to_all | solution.py:156
  112.8 6.0 %copy-start.28 = (f32[8,128,256]{2,1,0:T(8,128)S(1)}, f32[8,128,256]{2,1,0:T(8,128)}, u32[]{:S(2)}) copy-start(f32[8,128,256]{2,1,0:T(8,128)} %get-tuple-element.24) | copy-start | bytes 3145732
  118.8 8.7 %copy-start.13 = (f32[2048,256]{1,0:T(8,128)}, f32[2048,256]{1,0:T(8,128)S(1)}, u32[]{:S(2)}) copy-start(f32[2048,256]{1,0:T(8,128)S(1)} %fusion.136) | copy-start | bytes 6291460
  118.8 6.7 %copy-start.2 = (f32[1024,1024]{1,0:T(8,128)S(1)}, f32[1024,1024]{1,0:T(8,128)}, u32[]{:S(2)}) copy-start(f32[1024,1024]{1,0:T(8,128)} %constant.26) | copy-start | bytes 12582916
  125.5 2.2 copy-start.4
  138.6 28.7 %all-to-all-start.2 = ((f32[8,128,256]{2,1,0:T(8,128)}), f32[8,128,256]{2,1,0:T(8,128)}, u32[]{:S(2)}, u32[]{:S(2)}) async-start(f32[8,128,256]{2,1,0:T(8,128)} %bitcast.228), calls=%async_computation.2 | async-start | bytes 2097152 | tf_op jit(solution)/shard_map/all_to_all | solution.py:163
  143.1 6.4 %copy-start.3 = (f32[1024,1024]{1,0:T(8,128)S(1)}, f32[1024,1024]{1,0:T(8,128)}, u32[]{:S(2)}) copy-start(f32[1024,1024]{1,0:T(8,128)} %constant.26) | copy-start | bytes 12582916
  143.1 6.4 %copy-start.14 = (f32[2048,256]{1,0:T(8,128)S(1)}, f32[2048,256]{1,0:T(8,128)}, u32[]{:S(2)}) copy-start(f32[2048,256]{1,0:T(8,128)} %copy-done.13) | copy-start | bytes 6291460
  149.5 1.9 copy-start.11
  149.5 2.9 copy-start.5
  179.9 29.9 %all-to-all-start.3 = ((f32[8,128,256]{2,1,0:T(8,128)}), f32[8,128,256]{2,1,0:T(8,128)}, u32[]{:S(2)}, u32[]{:S(2)}) async-start(f32[8,128,256]{2,1,0:T(8,128)} %bitcast.227), calls=%async_computation.3 | async-start | bytes 2097152 | tf_op jit(solution)/shard_map/all_to_all | solution.py:163
  184.8 4.9 %copy-start.6 = (f32[1024,1024]{1,0:T(8,128)S(1)}, f32[1024,1024]{1,0:T(8,128)}, u32[]{:S(2)}) copy-start(f32[1024,1024]{1,0:T(8,128)} %constant.27) | copy-start | bytes 12582916
  184.8 4.9 %copy-start.12 = (f32[2048,256]{1,0:T(8,128)S(1)}, f32[2048,256]{1,0:T(8,128)}, u32[]{:S(2)}) copy-start(f32[2048,256]{1,0:T(8,128)} %copy-done.11) | copy-start | bytes 6291460
  189.7 3.0 copy-start.16
  189.7 3.0 copy-start.36
  209.8 12.1 %copy-start.17 = (f32[128,2048]{1,0:T(8,128)S(1)}, f32[128,2048]{1,0:T(8,128)}, u32[]{:S(2)}) copy-start(f32[128,2048]{1,0:T(8,128)} %param.23) | copy-start | bytes 3145732
  209.8 12.1 %copy-start.22 = (f32[128,2048]{1,0:T(8,128)S(1)}, f32[128,2048]{1,0:T(8,128)}, u32[]{:S(2)}) copy-start(f32[128,2048]{1,0:T(8,128)} %param.27) | copy-start | bytes 3145732
  209.8 29.8 %all-to-all-start.5 = ((f32[8,128,256]{2,1,0:T(8,128)}), f32[8,128,256]{2,1,0:T(8,128)}, u32[]{:S(2)}, u32[]{:S(2)}) async-start(f32[8,128,256]{2,1,0:T(8,128)} %bitcast.226), calls=%async_computation.5 | async-start | bytes 2097152 | tf_op jit(solution)/shard_map/all_to_all | solution.py:163
  214.4 7.5 %copy-start.27 = (f32[128,2048]{1,0:T(8,128)S(1)}, f32[128,2048]{1,0:T(8,128)}, u32[]{:S(2)}) copy-start(f32[128,2048]{1,0:T(8,128)} %get-tuple-element.30) | copy-start | bytes 3145732
  214.4 7.5 %copy-start.37 = (f32[128]{0:T(128)S(1)}, f32[128]{0:T(128)}, u32[]{:S(2)}) copy-start(f32[128]{0:T(128)} %copy-done.35) | copy-start | bytes 1540
  214.4 7.5 %copy-start.39 = (f32[128]{0:T(128)S(1)}, f32[128]{0:T(128)}, u32[]{:S(2)}) copy-start(f32[128]{0:T(128)} %get-tuple-element.28) | copy-start | bytes 1540
  214.5 7.5 %copy-start.40 = (f32[128]{0:T(128)S(1)}, f32[128]{0:T(128)}, u32[]{:S(2)}) copy-start(f32[128]{0:T(128)} %broadcast_multiply_fusion) | copy-start | bytes 1540
  222.0 3.2 copy-start.24
  225.1 1.2 copy-start.18
  225.3 1.9 copy-start.10
  239.6 32.9 %all-to-all-start.4 = ((f32[8,136,256]{2,1,0:T(8,128)}), f32[8,136,256]{2,1,0:T(8,128)}, u32[]{:S(2)}, u32[]{:S(2)}) async-start(f32[8,136,256]{2,1,0:T(8,128)} %bitcast_dynamic-update-slice_fusion), calls=%async_computation.4 | async-start | bytes 2228224 | tf_op jit(solution)/shard_map/all_to_all | solution.py:156
  243.8 70.4 %all-gather.2.cloned.1.call-start = ((), (), s32[]{:S(2)}) async-start(), calls=%async_computation.6 | async-start | bytes 1253376 | tf_op jit(solution)/shard_map/all_gather | solution.py:249
  248.6 32.2 %collective-permute-start.1 = (f32[128,2048]{1,0:T(8,128)S(1)}, f32[128,2048]{1,0:T(8,128)}, u32[]{:S(2)}, u32[]{:S(2)}) collective-permute-start(f32[128,2048]{1,0:T(8,128)S(1)} %mul.189), channel_id=1, source_target_pairs={{4,0},{8,4},{12,8},{16,12},{20,16},{24,20},{28,24},{5,1},{9,5},{13... | collective-permute-start | bytes 3145736 | tf_op jit(solution)/shard_map/ppermute | solution.py:14
  280.8 2.4 copy-start.8
  283.2 1.2 copy-start.19
  283.2 1.5 copy-start.21
  283.3 1.8 copy-start.26
  285.1 32.8 %copy-start.1 = (f32[128,2048]{1,0:T(8,128)S(1)}, f32[128,2048]{1,0:T(8,128)}, u32[]{:S(2)}) copy-start(f32[128,2048]{1,0:T(8,128)} %param.24) | copy-start | bytes 3145732
  (2 other events, 1.3 us)
Sparse Core Ops, SparseCore 0:
  274.6 39.5 all-gather.1
where the time goes:
time: 326 us; the launch traced here: 325 us
  waiting for transfers between devices  119 us (37%)
  starting transfers between devices  59.8 us (18%)
  local copies, waits for them, and re-layouts  55.5 us (17%)
  matrix products  50.2 us (15%)
  between operations  14.8 us (5%)
  other arithmetic  12.9 us (4%)
  blocking collectives  12.5 us (4%)
    unnamed x131, local copies, waits for them, and re-layouts  43 us
    ppermute x2, waiting for transfers between devices, shifted(): return lax.ppermute(shard, axis, pairs)  38.8 us
    all_to_all x2, starting transfers between devices, gather_tokens(): lax.all_to_all(pieces, 'ctx', split_axis=0, concat_axis=0)  33.8 us
    all_to_all x2, waiting for transfers between devices, gather_tokens(): lax.all_to_all(pieces, 'ctx', split_axis=0, concat_axis=0)  28.9 us
    all_gather x1, waiting for transfers between devices, shards(): sums = lax.all_gather(sums, 'ctx', axis=1, tiled=True)  26.9 us
    dot_general x8, matrix products, to_spec(): return jnp.dot(table, signal, precision=lax.Precision.HIGH)  25.6 us
    dot_general x12, matrix products, from_spec(): return jnp.dot(back_table, spec, precision=lax.Precision.HIGH)  24.6 us
    all_to_all x3, waiting for transfers between devices, scatter_tokens(): lax.all_to_all(pieces, 'ctx', split_axis=0, concat_axis=0)  24.3 us
  transfers between devices with their start and end apart: 9, of which 7 were waited for; matrix products, arithmetic and copies ran while one was open for 26% of the time, Pallas kernels for 0%

commit v1 on v0

--- a/solution.py
+++ b/solution.py
@@ -146,9 +146,10 @@
 
 def by_groups(array):
     groups = lax.axis_size("ctx")
-    width = array.shape[1] // groups
-    array = rows_first(array)
-    return jnp.stack([array[:, i * width : (i + 1) * width] for i in range(groups)])
+    rows, columns = array.shape
+    strip = math.gcd(rows, 8)
+    strips = rows_first(array).reshape(rows // strip, strip, groups, columns // groups)
+    return strips.transpose(2, 0, 1, 3).reshape(groups, rows, columns // groups)
 
 
 def gather_tokens(array):
@@ -161,11 +162,11 @@
     groups = lax.axis_size("ctx")
     pieces = rows_first(rows_first(array).reshape(groups, -1, array.shape[1]))
     pieces = rows_first(lax.all_to_all(pieces, "ctx", split_axis=0, concat_axis=0))
-    return rows_first(jnp.concatenate([pieces[i] for i in range(groups)], 1))
-
-
-def after(array, *earlier):
-    return lax.optimization_barrier((array, *earlier))[0]
+    return rows_first(pieces.transpose(1, 0, 2).reshape(pieces.shape[1], -1))
+
+
+def after(array, earlier):
+    return array + 0.0 * earlier[0, 0]
 
 
 def both_tokens(first, second):
@@ -208,7 +209,7 @@
     dense = 8 * length * length <= DENSE_TABLE_BYTES
     if dense:
         table = half_step_table(2 * length, length)
-        filt_all, grad_all = both_tokens(filter_lr, grad_conv_lr)
+        filt_all, grad_all = both_tokens(filter_lr, after(grad_conv_lr, preceding))
     residual = layer_in + query_mr * conv_mr
     square_sum = lax.psum(jnp.sum(residual * residual, axis=1), "chan")
     inv_rms = lax.rsqrt(square_sum / full_width + 1e-06)[:, None]
@@ -222,7 +223,7 @@
         grad_long_in = scatter_tokens(after(back_all, val_all))
         long_val = to_spec(table, val_all)
         conv_all = from_spec(table, times(long_val, long_filt))
-        conv_lr = scatter_tokens(after(conv_all, grad_long_in))
+        conv_lr = scatter_tokens(conv_all)
     else:
         conv_lr, grad_long_in, grad_filter_lr = split_long_pass(long_in, grad_conv_lr, filter_lr)
     grad_query_lr = out_grad * conv_lr
@@ -241,7 +242,7 @@
     filter_part = from_spec(tap_table, conj_times(mixed_spec, own_spec))
     spare = jnp.zeros((-(tap_count + 1) % 8, chan_count), jnp.float32)
     parts = jnp.concatenate([filter_part, gain_part[None], spare], 0)
-    parts = gather_tokens(after(parts, conv_lr))
+    parts = gather_tokens(parts)
     sums = jnp.sum(parts.reshape(lax.axis_size("ctx"), -1, parts.shape[1]), axis=0)
     if dense:
         filt_all = from_spec(table, conj_times(long_val, long_grad))

time: 326 us -> 326 us (level)
  waiting for transfers between devices: 119 us -> 168 us
  local copies, waits for them, and re-layouts: 55.5 us -> 23.7 us
  starting transfers between devices: 59.8 us -> 35.7 us
  matrix products: 50.2 us -> 53.7 us
    all_to_all x3, waiting for transfers between devices: 24.3 us -> 71.5 us  [scatter_tokens(): lax.all_to_all(pieces, 'ctx', split_axis=0, concat_axis=0)]
    unnamed x131 -> x72, local copies, waits for them, and re-layouts: 43 us -> 4.74 us
    all_to_all x1, waiting for transfers between devices: 0.01 us -> 33.5 us  [both_tokens(): lax.all_to_all(pieces, 'ctx', split_axis=0, concat_axis=0)]
    all_gather x1, waiting for transfers between devices: 26.9 us -> 0.01 us  [shards(): sums = lax.all_gather(sums, 'ctx', axis=1, tiled=True)]
    all_to_all x2, starting transfers between devices: 33.8 us -> 9 us  [gather_tokens(): lax.all_to_all(pieces, 'ctx', split_axis=0, concat_axis=0)]
    ppermute x2, waiting for transfers between devices: 38.8 us -> 22.3 us  [shifted(): return lax.ppermute(shard, axis, pairs)]
    all_to_all x2, waiting for transfers between devices: 28.9 us -> 40.8 us  [gather_tokens(): lax.all_to_all(pieces, 'ctx', split_axis=0, concat_axis=0)]
    reshape x0 -> x6, local copies, waits for them, and re-layouts: none -> 8.51 us  [the longest x3 6.11 us: scatter_tokens(): return rows_first(pieces.transpose(1, 0, 2).reshape(pieces.shape[1], -1))]
  transfers between devices with their start and end apart: 9 -> 9, of which waited for: 7 -> 7; matrix products, arithmetic and copies ran while one was open for 26% -> 15% of each run, Pallas kernels for 0% -> 0%
where the time goes in v1:
time: 326 us; the launch traced here: 325 us
  waiting for transfers between devices  168 us (52%)
  matrix products  53.7 us (16%)
  starting transfers between devices  35.7 us (11%)
  local copies, waits for them, and re-layouts  23.7 us (7%)
  between operations  17.2 us (5%)
  other arithmetic  14.3 us (4%)
  blocking collectives  12.3 us (4%)
    all_to_all x3, waiting for transfers between devices, scatter_tokens(): lax.all_to_all(pieces, 'ctx', split_axis=0, concat_axis=0)  71.5 us
    all_to_all x2, waiting for transfers between devices, gather_tokens(): lax.all_to_all(pieces, 'ctx', split_axis=0, concat_axis=0)  40.8 us
    all_to_all x1, waiting for transfers between devices, both_tokens(): lax.all_to_all(pieces, 'ctx', split_axis=0, concat_axis=0)  33.5 us
    dot_general x12, matrix products, from_spec(): return jnp.dot(back_table, spec, precision=lax.Precision.HIGH)  28.3 us
    dot_general x8, matrix products, to_spec(): return jnp.dot(table, signal, precision=lax.Precision.HIGH)  25.4 us
    ppermute x2, waiting for transfers between devices, shifted(): return lax.ppermute(shard, axis, pairs)  22.3 us
    all_to_all x3, starting transfers between devices, scatter_tokens(): lax.all_to_all(pieces, 'ctx', split_axis=0, concat_axis=0)  13.1 us
    all_to_all x2, starting transfers between devices, gather_tokens(): lax.all_to_all(pieces, 'ctx', split_axis=0, concat_axis=0)  9 us
  transfers between devices with their start and end apart: 9, of which 7 were waited for; matrix products, arithmetic and copies ran while one was open for 15% of the time, Pallas kernels for 0%

profile of v1, /device:TPU:0, one launch (start us, length us, event | category | flops | bytes accessed | tf_op | source)
XLA Modules:
  0.0 324.9 jit_solution(6639095930719740800)
XLA Ops:
  7.2 1.8 mul.188
  9.0 5.1 %collective-permute-start = (f32[128,2048]{1,0:T(8,128)S(1)}, f32[128,2048]{1,0:T(8,128)S(1)}, u32[]{:S(2)}, u32[]{:S(2)}) collective-permute-start(f32[128,2048]{1,0:T(8,128)S(1)} %mul.188), channel_id=1, source_target_pairs={{0,4},{4,8},{8,12},{12,16},{16,20},{20,24},{24,28},{1,5},{5,9},{9,... | collective-permute-start | bytes 3145736 | tf_op jit(solution)/shard_map/ppermute | solution.py:14
  14.1 22.3 %collective-permute-done = f32[128,2048]{1,0:T(8,128)S(1)} collective-permute-done((f32[128,2048]{1,0:T(8,128)S(1)}, f32[128,2048]{1,0:T(8,128)S(1)}, u32[]{:S(2)}, u32[]{:S(2)}) %collective-permute-start) | collective-permute-done | bytes 1048608 | tf_op jit(solution)/shard_map/ppermute | solution.py:14
  38.0 1.6 pad_maximum_fusion
  39.6 6.9 %all-to-all-start = ((f32[8,256,256]{2,1,0:T(8,128)}), f32[8,256,256]{2,1,0:T(8,128)}, u32[]{:S(2)}, u32[]{:S(2)}) async-start(f32[8,256,256]{2,1,0:T(8,128)} %pad_maximum_fusion), calls=%async_computation | async-start | bytes 4194304 | tf_op jit(solution)/shard_map/all_to_all | solution.py:174
  46.5 1.0 fusion.100
  47.6 1.0 fusion.101
  48.7 1.0 fusion
  50.4 1.3 copy-done.20
  52.0 1.9 multiply_reduce_fusion.2
  53.9 6.0 %psum.14 = f32[128]{0:T(128)S(1)} all-reduce(f32[128]{0:T(128)S(1)} %get-tuple-element.12), channel_id=1, replica_groups=mesh['ctx'=8,'chan'=4] {'chan'}, use_global_device_ids=true, to_apply=%region_1.0 | all-reduce | flops 128 | bytes 1024 | tf_op jit(solution)/shard_map/psum | solution.py:214
  60.5 33.5 %all-to-all-done = f32[8,256,256]{2,1,0:T(8,128)} async-done(((f32[8,256,256]{2,1,0:T(8,128)}), f32[8,256,256]{2,1,0:T(8,128)}, u32[]{:S(2)}, u32[]{:S(2)}) %all-to-all-start) | async-done | bytes 2097184 | tf_op jit(solution)/shard_map/all_to_all | solution.py:174
  94.0 2.6 fusion.98
  98.1 1.1 copy.59
  99.1 4.4 %all-to-all-start.1 = ((f32[8,128,256]{2,1,0:T(8,128)}), f32[8,128,256]{2,1,0:T(8,128)}, u32[]{:S(2)}, u32[]{:S(2)}) async-start(f32[8,128,256]{2,1,0:T(8,128)} %bitcast.85), calls=%async_computation.1 | async-start | bytes 2097152 | tf_op jit(solution)/shard_map/all_to_all | solution.py:157
  103.6 6.2 %fusion.102 = f32[2048,256]{1,0:T(8,128)S(1)} fusion(f32[2048,1024]{1,0:T(8,128)} %constant.27.clone, f32[1024,256]{1,0:T(8,128)} %bitcast.98), kind=kOutput, calls=%fused_computation.128 | convolution fusion | flops 3221225472 | bytes 11534336 | tf_op jit(solution)/shard_map/dot_general | solution.py:123
  109.8 19.3 %all-to-all-done.1 = f32[8,128,256]{2,1,0:T(8,128)} async-done(((f32[8,128,256]{2,1,0:T(8,128)}), f32[8,128,256]{2,1,0:T(8,128)}, u32[]{:S(2)}, u32[]{:S(2)}) %all-to-all-start.1) | async-done | bytes 1048608 | tf_op jit(solution)/shard_map/all_to_all | solution.py:157
  129.1 6.4 %fusion.105 = f32[2048,256]{1,0:T(8,128)S(1)} fusion(f32[2048,1024]{1,0:T(8,128)} %constant.27.clone, f32[1024,256]{1,0:T(8,128)} %bitcast.15), kind=kOutput, calls=%fused_computation.131 | convolution fusion | flops 3221225472 | bytes 11534336 | tf_op jit(solution)/shard_map/dot_general | solution.py:123
  135.5 2.0 fusion.16
  138.4 3.0 convolution_add_fusion.5
  141.4 4.5 %all-to-all-start.4 = ((f32[8,128,256]{2,1,0:T(8,128)}), f32[8,128,256]{2,1,0:T(8,128)}, u32[]{:S(2)}, u32[]{:S(2)}) async-start(f32[8,128,256]{2,1,0:T(8,128)} %bitcast.95), calls=%async_computation.4 | async-start | bytes 2097152 | tf_op jit(solution)/shard_map/all_to_all | solution.py:164
  145.9 6.3 %fusion.103 = f32[2048,256]{1,0:T(8,128)S(1)} fusion(f32[2048,1024]{1,0:T(8,128)} %constant.27.clone, f32[1024,256]{1,0:T(8,128)} %bitcast.96), kind=kOutput, calls=%fused_computation.129 | convolution fusion | flops 3221225472 | bytes 11534336 | tf_op jit(solution)/shard_map/dot_general | solution.py:123
  152.3 2.0 fusion.37
  154.3 1.2 slice.122
  156.1 3.0 fusion.5
  159.1 12.0 %all-to-all-done.4 = f32[8,128,256]{2,1,0:T(8,128)} async-done(((f32[8,128,256]{2,1,0:T(8,128)}), f32[8,128,256]{2,1,0:T(8,128)}, u32[]{:S(2)}, u32[]{:S(2)}) %all-to-all-start.4) | async-done | bytes 1048608 | tf_op jit(solution)/shard_map/all_to_all | solution.py:164
  171.1 4.2 %all-to-all-start.2 = ((f32[8,128,256]{2,1,0:T(8,128)}), f32[8,128,256]{2,1,0:T(8,128)}, u32[]{:S(2)}, u32[]{:S(2)}) async-start(f32[8,128,256]{2,1,0:T(8,128)} %bitcast.92), calls=%async_computation.2 | async-start | bytes 2097152 | tf_op jit(solution)/shard_map/all_to_all | solution.py:164
  176.0 2.3 copy.52
  178.3 22.4 %all-to-all-done.2 = f32[8,128,256]{2,1,0:T(8,128)} async-done(((f32[8,128,256]{2,1,0:T(8,128)}), f32[8,128,256]{2,1,0:T(8,128)}, u32[]{:S(2)}, u32[]{:S(2)}) %all-to-all-start.2) | async-done | bytes 1048608 | tf_op jit(solution)/shard_map/all_to_all | solution.py:164
  200.7 1.4 copy.51
  202.3 2.7 multiply_reduce_fusion
  204.9 6.3 %psum.15 = f32[128]{0:T(128)} all-reduce(f32[128]{0:T(128)} %get-tuple-element.9), channel_id=1, replica_groups=mesh['ctx'=8,'chan'=4] {'chan'}, use_global_device_ids=true, to_apply=%region_3.0 | all-reduce | flops 128 | bytes 1024 | tf_op jit(solution)/shard_map/psum | solution.py:234
  211.9 4.4 %fusion.97 = (f32[128,2048]{1,0:T(8,128)}, f32[128,2048]{1,0:T(8,128)S(1)}, f32[128,2048]{1,0:T(8,128)}) fusion(f32[128,2048]{1,0:T(8,128)} %get-tuple-element.22, f32[128]{0:T(128)S(1)} %broadcast_multiply_fusion, f32[128,2048]{1,0:T(8,128)S(1)} %get-tuple-element.13, f32[128]{0:T(128)} %get-tuple-element.20, f32[128,2048]{1,0:T(8,128)} %param.27, ...), kind=kLoop, calls=%fused_computation.123 | loop fusion | flops 2359296 | bytes 9446912 | tf_op jit(solution)/shard_map/mul | solution.py:238
  219.7 1.1 copy.58
  220.9 4.6 %all-to-all-start.3 = ((f32[8,136,256]{2,1,0:T(8,128)}), f32[8,136,256]{2,1,0:T(8,128)}, u32[]{:S(2)}, u32[]{:S(2)}) async-start(f32[8,136,256]{2,1,0:T(8,128)} %bitcast.88), calls=%async_computation.3 | async-start | bytes 2228224 | tf_op jit(solution)/shard_map/all_to_all | solution.py:157
  225.8 5.7 %fusion.9 = f32[256,1024]{0,1:T(8,128)} fusion(f32[1024,1024]{1,0:T(8,128)} %constant.31, f32[2048,256]{1,0:T(8,128)} %copy-done.6, f32[2048,256]{1,0:T(8,128)S(1)} %fusion.103), kind=kOutput, calls=%fused_computation.23 | convolution fusion | flops 1611399168 | bytes 9437184 | tf_op jit(solution)/shard_map/dot_general | solution.py:128
  231.4 1.3 collective-permute-start.1
  232.7 21.5 %all-to-all-done.3 = f32[8,136,256]{2,1,0:T(8,128)} async-done(((f32[8,136,256]{2,1,0:T(8,128)}), f32[8,136,256]{2,1,0:T(8,128)}, u32[]{:S(2)}, u32[]{:S(2)}) %all-to-all-start.3) | async-done | bytes 1114144 | tf_op jit(solution)/shard_map/all_to_all | solution.py:157
  254.2 1.2 slice.131
  256.1 2.0 reduce_sum.39
  258.1 5.9 %fusion.4 = f32[256,1024]{0,1:T(8,128)} fusion(f32[256,1024]{0,1:T(8,128)} %fusion.9, f32[1024,1024]{1,0:T(8,128)} %constant.32, f32[2048,256]{1,0:T(8,128)} %copy-done.6, f32[2048,256]{1,0:T(8,128)S(1)} %fusion.103, f32[]{:T(128)} %bitcast.31), kind=kOutput, calls=%fused_computation.11 | convolution fusion | flops 1611923456 | bytes 10485764 | tf_op jit(solution)/shard_map/dot_general | solution.py:128
  264.0 4.4 %all-to-all-start.5 = ((f32[8,128,256]{2,1,0:T(8,128)}), f32[8,128,256]{2,1,0:T(8,128)}, u32[]{:S(2)}, u32[]{:S(2)}) async-start(f32[8,128,256]{2,1,0:T(8,128)} %bitcast.90), calls=%async_computation.5 | async-start | bytes 2097152 | tf_op jit(solution)/shard_map/all_to_all | solution.py:164
  268.4 2.4 convolution_add_fusion
  272.7 2.2 fusion.99
  274.9 37.0 %all-to-all-done.5 = f32[8,128,256]{2,1,0:T(8,128)} async-done(((f32[8,128,256]{2,1,0:T(8,128)}), f32[8,128,256]{2,1,0:T(8,128)}, u32[]{:S(2)}, u32[]{:S(2)}) %all-to-all-start.5) | async-done | bytes 1048608 | tf_op jit(solution)/shard_map/all_to_all | solution.py:164
  311.9 2.4 copy.53
  314.3 2.3 slice.127
  316.6 1.4 slice.128
  (91 shorter events, 11.2 us)
Async XLA Ops:
  7.2 40.4 %copy-start = (f32[128,2048]{1,0:T(8,128)S(1)}, f32[128,2048]{1,0:T(8,128)}, u32[]{:S(2)}) copy-start(f32[128,2048]{1,0:T(8,128)} %param.24) | copy-start | bytes 3145732
  7.2 30.4 %copy-start.28 = (f32[128,2048]{1,0:T(8,128)S(1)}, f32[128,2048]{1,0:T(8,128)}, u32[]{:S(2)}) copy-start(f32[128,2048]{1,0:T(8,128)} %param.22) | copy-start | bytes 3145732
  7.2 30.4 %copy-start.22 = (f32[128,2048]{1,0:T(8,128)S(1)}, f32[128,2048]{1,0:T(8,128)}, u32[]{:S(2)}) copy-start(f32[128,2048]{1,0:T(8,128)} %param.27) | copy-start | bytes 3145732
  9.0 28.7 %copy-start.29 = (f32[128,2048]{1,0:T(8,128)S(1)}, f32[128,2048]{1,0:T(8,128)}, u32[]{:S(2)}) copy-start(f32[128,2048]{1,0:T(8,128)} %param.25) | copy-start | bytes 3145732
  9.0 27.4 %collective-permute-start = (f32[128,2048]{1,0:T(8,128)S(1)}, f32[128,2048]{1,0:T(8,128)S(1)}, u32[]{:S(2)}, u32[]{:S(2)}) collective-permute-start(f32[128,2048]{1,0:T(8,128)S(1)} %mul.188), channel_id=1, source_target_pairs={{0,4},{4,8},{8,12},{12,16},{16,20},{20,24},{24,28},{1,5},{5,9},{9,... | collective-permute-start | bytes 3145736 | tf_op jit(solution)/shard_map/ppermute | solution.py:14
  39.6 6.9 %copy-start.27 = (f32[256,128]{1,0:T(8,128)S(1)}, f32[256,128]{1,0:T(8,128)}, u32[]{:S(2)}) copy-start(f32[256,128]{1,0:T(8,128)} %constant.24.clone) | copy-start | bytes 393220
  39.6 54.4 %all-to-all-start = ((f32[8,256,256]{2,1,0:T(8,128)}), f32[8,256,256]{2,1,0:T(8,128)}, u32[]{:S(2)}, u32[]{:S(2)}) async-start(f32[8,256,256]{2,1,0:T(8,128)} %pad_maximum_fusion), calls=%async_computation | async-start | bytes 4194304 | tf_op jit(solution)/shard_map/all_to_all | solution.py:174
  47.6 1.0 copy-start.32
  48.6 1.8 copy-start.11
  48.6 1.1 copy-start.31
  49.7 4.2 %copy-start.13 = (f32[256,2048]{0,1:T(8,128)}, f32[256,2048]{0,1:T(8,128)S(1)}, u32[]{:S(2)}) copy-start(f32[256,2048]{0,1:T(8,128)S(1)} %fusion) | copy-start | bytes 6291460
  49.7 2.0 copy-start.20
  49.7 2.3 copy-start.23
  49.7 2.3 copy-start.30
  60.5 37.4 %copy-start.34 = (f32[128]{0:T(128)}, f32[128]{0:T(128)S(1)}, u32[]{:S(2)}) copy-start(f32[128]{0:T(128)S(1)} %get-tuple-element.21) | copy-start | bytes 1540
  60.5 37.4 %copy-start.15 = (f32[128,2048]{1,0:T(8,128)S(1)}, f32[128,2048]{1,0:T(8,128)}, u32[]{:S(2)}) copy-start(f32[128,2048]{1,0:T(8,128)} %param.23) | copy-start | bytes 3145732
  60.5 37.4 %copy-start.33 = (f32[2048]{0:T(1024)S(1)}, f32[2048]{0:T(1024)}, u32[]{:S(2)}) copy-start(f32[2048]{0:T(1024)} %param.26) | copy-start | bytes 24580
  96.6 2.5 copy-start.26
  99.1 29.9 %all-to-all-start.1 = ((f32[8,128,256]{2,1,0:T(8,128)}), f32[8,128,256]{2,1,0:T(8,128)}, u32[]{:S(2)}, u32[]{:S(2)}) async-start(f32[8,128,256]{2,1,0:T(8,128)} %bitcast.85), calls=%async_computation.1 | async-start | bytes 2097152 | tf_op jit(solution)/shard_map/all_to_all | solution.py:157
  109.7 27.7 %copy-start.9 = (f32[2048,256]{1,0:T(8,128)}, f32[2048,256]{1,0:T(8,128)S(1)}, u32[]{:S(2)}) copy-start(f32[2048,256]{1,0:T(8,128)S(1)} %fusion.102) | copy-start | bytes 6291460
  129.1 6.4 %copy-start.2 = (f32[1024,1024]{1,0:T(8,128)S(1)}, f32[1024,1024]{1,0:T(8,128)}, u32[]{:S(2)}) copy-start(f32[1024,1024]{1,0:T(8,128)} %constant.31) | copy-start | bytes 12582916
  135.4 2.0 copy-start.6
  135.5 2.9 copy-start.4
  141.4 29.6 %all-to-all-start.4 = ((f32[8,128,256]{2,1,0:T(8,128)}), f32[8,128,256]{2,1,0:T(8,128)}, u32[]{:S(2)}, u32[]{:S(2)}) async-start(f32[8,128,256]{2,1,0:T(8,128)} %bitcast.95), calls=%async_computation.4 | async-start | bytes 2097152 | tf_op jit(solution)/shard_map/all_to_all | solution.py:164
  145.9 6.3 %copy-start.3 = (f32[1024,1024]{1,0:T(8,128)S(1)}, f32[1024,1024]{1,0:T(8,128)}, u32[]{:S(2)}) copy-start(f32[1024,1024]{1,0:T(8,128)} %constant.31) | copy-start | bytes 12582916
  145.9 6.3 %copy-start.10 = (f32[2048,256]{1,0:T(8,128)S(1)}, f32[2048,256]{1,0:T(8,128)}, u32[]{:S(2)}) copy-start(f32[2048,256]{1,0:T(8,128)} %copy-done.9) | copy-start | bytes 6291460
  152.3 3.8 %copy-start.5 = (f32[1024,1024]{1,0:T(8,128)S(1)}, f32[1024,1024]{1,0:T(8,128)}, u32[]{:S(2)}) copy-start(f32[1024,1024]{1,0:T(8,128)} %constant.32) | copy-start | bytes 12582916
  171.1 29.6 %all-to-all-start.2 = ((f32[8,128,256]{2,1,0:T(8,128)}), f32[8,128,256]{2,1,0:T(8,128)}, u32[]{:S(2)}, u32[]{:S(2)}) async-start(f32[8,128,256]{2,1,0:T(8,128)} %bitcast.92), calls=%async_computation.2 | async-start | bytes 2097152 | tf_op jit(solution)/shard_map/all_to_all | solution.py:164
  200.7 1.5 copy-start.16
  202.1 2.8 copy-start.17
  211.9 4.4 %copy-start.24 = (f32[128,2048]{1,0:T(8,128)S(1)}, f32[128,2048]{1,0:T(8,128)}, u32[]{:S(2)}) copy-start(f32[128,2048]{1,0:T(8,128)} %param.20) | copy-start | bytes 3145732
  216.2 1.2 copy-start.18
  216.3 1.9 copy-start.14
  218.2 1.4 copy-start.7
  218.9 0.7 copy-start.35
  220.9 33.3 %all-to-all-start.3 = ((f32[8,136,256]{2,1,0:T(8,128)}), f32[8,136,256]{2,1,0:T(8,128)}, u32[]{:S(2)}, u32[]{:S(2)}) async-start(f32[8,136,256]{2,1,0:T(8,128)} %bitcast.88), calls=%async_computation.3 | async-start | bytes 2228224 | tf_op jit(solution)/shard_map/all_to_all | solution.py:157
  225.4 88.9 %all-gather.2.cloned.1.call-start = ((), (), s32[]{:S(2)}) async-start(), calls=%async_computation.6 | async-start | bytes 1253376 | tf_op jit(solution)/shard_map/all_gather | solution.py:250
  231.4 36.9 %collective-permute-start.1 = (f32[128,2048]{1,0:T(8,128)S(1)}, f32[128,2048]{1,0:T(8,128)}, u32[]{:S(2)}, u32[]{:S(2)}) collective-permute-start(f32[128,2048]{1,0:T(8,128)S(1)} %mul.219), channel_id=1, source_target_pairs={{4,0},{8,4},{12,8},{16,12},{20,16},{24,20},{28,24},{5,1},{9,5},{13... | collective-permute-start | bytes 3145736 | tf_op jit(solution)/shard_map/ppermute | solution.py:14
  264.0 4.4 %copy-start.8 = (f32[256,2048]{0,1:T(8,128)S(1)}, f32[256,2048]{0,1:T(8,128)}, u32[]{:S(2)}) copy-start(f32[256,2048]{0,1:T(8,128)} %copy-done.7) | copy-start | bytes 6291460
  264.0 48.0 %all-to-all-start.5 = ((f32[8,128,256]{2,1,0:T(8,128)}), f32[8,128,256]{2,1,0:T(8,128)}, u32[]{:S(2)}, u32[]{:S(2)}) async-start(f32[8,128,256]{2,1,0:T(8,128)} %bitcast.90), calls=%async_computation.5 | async-start | bytes 2097152 | tf_op jit(solution)/shard_map/all_to_all | solution.py:164
  268.4 2.5 copy-start.12
  270.8 1.2 copy-start.19
  270.8 1.5 copy-start.21
  270.9 1.8 copy-start.25
  311.9 6.1 %copy-start.1 = (f32[128,2048]{1,0:T(8,128)S(1)}, f32[128,2048]{1,0:T(8,128)}, u32[]{:S(2)}) copy-start(f32[128,2048]{1,0:T(8,128)} %param.24) | copy-start | bytes 3145732
Sparse Core Ops, SparseCore 0:
  258.2 51.9 all-gather.1

commit v2 on v1

--- a/solution.py
+++ b/solution.py
@@ -203,30 +203,27 @@
     grad_conv_lr = out_grad * query_lr
     mixed_in = key_mr * layer_in
     preceding = shifted(mixed_in[row_count - tap_count :], "ctx", 1)
+    dense = 8 * length * length <= DENSE_TABLE_BYTES
+    if dense:
+        table = half_step_table(2 * length, length)
+        filt_all, grad_all = both_tokens(filter_lr, grad_conv_lr)
+        long_filt = to_spec(table, filt_all)
+        long_grad = to_spec(table, grad_all)
+        back_all = from_spec(table, conj_times(long_filt, long_grad))
+        grad_long_in = scatter_tokens(back_all)
+        preceding = after(preceding, back_all)
     filt_spec = to_spec(tap_table, filter_mr)
     mixed_spec = to_spec(own_table, mixed_in) - to_spec(next_table, preceding)
     conv_mr = from_spec(own_table, times(mixed_spec, filt_spec))
-    dense = 8 * length * length <= DENSE_TABLE_BYTES
-    if dense:
-        table = half_step_table(2 * length, length)
-        filt_all, grad_all = both_tokens(filter_lr, after(grad_conv_lr, preceding))
     residual = layer_in + query_mr * conv_mr
     square_sum = lax.psum(jnp.sum(residual * residual, axis=1), "chan")
     inv_rms = lax.rsqrt(square_sum / full_width + 1e-06)[:, None]
     normed = residual * inv_rms * norm_gain
     long_in = key_lr * normed
     if dense:
-        val_all = gather_tokens(after(long_in, filt_all))
-        long_filt = to_spec(table, filt_all)
-        long_grad = to_spec(table, grad_all)
-        back_all = from_spec(table, conj_times(long_filt, long_grad))
-        grad_long_in = scatter_tokens(after(back_all, val_all))
-        long_val = to_spec(table, val_all)
-        conv_all = from_spec(table, times(long_val, long_filt))
-        conv_lr = scatter_tokens(conv_all)
+        val_all = gather_tokens(after(long_in, grad_long_in))
     else:
         conv_lr, grad_long_in, grad_filter_lr = split_long_pass(long_in, grad_conv_lr, filter_lr)
-    grad_query_lr = out_grad * conv_lr
     grad_key_lr = grad_long_in * normed
     grad_normed = grad_long_in * key_lr
     gain_part = jnp.sum(grad_normed * residual * inv_rms, axis=0)
@@ -242,11 +239,17 @@
     filter_part = from_spec(tap_table, conj_times(mixed_spec, own_spec))
     spare = jnp.zeros((-(tap_count + 1) % 8, chan_count), jnp.float32)
     parts = jnp.concatenate([filter_part, gain_part[None], spare], 0)
-    parts = gather_tokens(parts)
-    sums = jnp.sum(parts.reshape(lax.axis_size("ctx"), -1, parts.shape[1]), axis=0)
-    if dense:
+    if dense:
+        parts = after(parts, val_all)
+        long_val = to_spec(table, after(val_all, parts))
+    totals = gather_tokens(parts)
+    sums = jnp.sum(totals.reshape(lax.axis_size("ctx"), -1, totals.shape[1]), axis=0)
+    if dense:
+        conv_all = from_spec(table, times(long_val, long_filt))
+        conv_lr = scatter_tokens(after(conv_all, totals))
         filt_all = from_spec(table, conj_times(long_val, long_grad))
-        grad_filter_lr = scatter_tokens(after(filt_all, parts))
+        grad_filter_lr = scatter_tokens(after(filt_all, conv_lr))
+    grad_query_lr = out_grad * conv_lr
     sums = lax.all_gather(sums, "ctx", axis=1, tiled=True)
     grad_filter_mr, grad_gain = sums[:tap_count], sums[tap_count]
     grad_spec = own_spec + to_spec(next_table, following)

time: 326 us -> 293 us (0.90)
  waiting for transfers between devices: 168 us -> 125 us
  matrix products: 53.7 us -> 57.8 us
    all_to_all x3, waiting for transfers between devices: 71.5 us -> 41.8 us  [scatter_tokens(): lax.all_to_all(pieces, 'ctx', split_axis=0, concat_axis=0)]
    ppermute x2, waiting for transfers between devices: 22.3 us -> 0.01 us  [shifted(): return lax.ppermute(shard, axis, pairs)]
    all_to_all x2, waiting for transfers between devices: 40.8 us -> 23.7 us  [gather_tokens(): lax.all_to_all(pieces, 'ctx', split_axis=0, concat_axis=0)]
    all_gather x1, waiting for transfers between devices: 0.01 us -> 16.1 us  [shards(): sums = lax.all_gather(sums, 'ctx', axis=1, tiled=True)]
    all_to_all x1, waiting for transfers between devices: 33.5 us -> 43 us  [both_tokens(): lax.all_to_all(pieces, 'ctx', split_axis=0, concat_axis=0)]
    dot_general x12, matrix products: 28.3 us -> 33.2 us  [from_spec(): return jnp.dot(back_table, spec, precision=lax.Precision.HIGH)]
  transfers between devices with their start and end apart: 9 -> 9, of which waited for: 7 -> 7; matrix products, arithmetic and copies ran while one was open for 15% -> 24% of each run, Pallas kernels for 0% -> 0%
where the time goes in v2:
time: 293 us; the launch traced here: 291 us
  waiting for transfers between devices  125 us (43%)
  matrix products  57.8 us (20%)
  starting transfers between devices  35.6 us (12%)
  local copies, waits for them, and re-layouts  24.7 us (8%)
  between operations  18.5 us (6%)
  other arithmetic  17.4 us (6%)
  blocking collectives  12.8 us (4%)
    all_to_all x1, waiting for transfers between devices, both_tokens(): lax.all_to_all(pieces, 'ctx', split_axis=0, concat_axis=0)  43 us
    all_to_all x3, waiting for transfers between devices, scatter_tokens(): lax.all_to_all(pieces, 'ctx', split_axis=0, concat_axis=0)  41.8 us
    dot_general x12, matrix products, from_spec(): return jnp.dot(back_table, spec, precision=lax.Precision.HIGH)  33.2 us
    dot_general x8, matrix products, to_spec(): return jnp.dot(table, signal, precision=lax.Precision.HIGH)  24.5 us
    all_to_all x2, waiting for transfers between devices, gather_tokens(): lax.all_to_all(pieces, 'ctx', split_axis=0, concat_axis=0)  23.7 us
    all_gather x1, waiting for transfers between devices, shards(): sums = lax.all_gather(sums, 'ctx', axis=1, tiled=True)  16.1 us
    all_to_all x3, starting transfers between devices, scatter_tokens(): lax.all_to_all(pieces, 'ctx', split_axis=0, concat_axis=0)  14.2 us
    all_to_all x2, starting transfers between devices, gather_tokens(): lax.all_to_all(pieces, 'ctx', split_axis=0, concat_axis=0)  8.72 us
  transfers between devices with their start and end apart: 9, of which 7 were waited for; matrix products, arithmetic and copies ran while one was open for 24% of the time, Pallas kernels for 0%

profile of v2, /device:TPU:0, one launch (start us, length us, event | category | flops | bytes accessed | tf_op | source)
XLA Modules:
  0.0 291.5 jit_solution(12303211260850589897)
XLA Ops:
  7.2 1.8 mul.201
  9.3 1.5 pad_maximum_fusion
  10.9 7.4 %all-to-all-start = ((f32[8,256,256]{2,1,0:T(8,128)}), f32[8,256,256]{2,1,0:T(8,128)}, u32[]{:S(2)}, u32[]{:S(2)}) async-start(f32[8,256,256]{2,1,0:T(8,128)} %pad_maximum_fusion), calls=%async_computation | async-start | bytes 4194304 | tf_op jit(solution)/shard_map/all_to_all | solution.py:174
  18.3 1.3 mul.200
  19.6 4.0 %collective-permute-start = (f32[128,2048]{1,0:T(8,128)S(1)}, f32[128,2048]{1,0:T(8,128)S(1)}, u32[]{:S(2)}, u32[]{:S(2)}) collective-permute-start(f32[128,2048]{1,0:T(8,128)S(1)} %mul.200), channel_id=1, source_target_pairs={{0,4},{4,8},{8,12},{12,16},{16,20},{20,24},{24,28},{1,5},{5,9},{9,... | collective-permute-start | bytes 3145736 | tf_op jit(solution)/shard_map/ppermute | solution.py:14
  23.6 43.0 %all-to-all-done = f32[8,256,256]{2,1,0:T(8,128)} async-done(((f32[8,256,256]{2,1,0:T(8,128)}), f32[8,256,256]{2,1,0:T(8,128)}, u32[]{:S(2)}, u32[]{:S(2)}) %all-to-all-start) | async-done | bytes 2097184 | tf_op jit(solution)/shard_map/all_to_all | solution.py:174
  66.7 1.8 fusion.103
  68.5 6.7 %fusion.107 = f32[2048,256]{1,0:T(8,128)S(1)} fusion(f32[2048,1024]{1,0:T(8,128)} %constant.26.clone, f32[1024,256]{1,0:T(8,128)S(1)} %bitcast.100), kind=kOutput, calls=%fused_computation.132 | convolution fusion | flops 3221225472 | bytes 11534336 | tf_op jit(solution)/shard_map/dot_general | solution.py:123
  75.3 3.7 %fusion.106 = f32[2048,256]{1,0:T(8,128)S(1)} fusion(f32[2048,1024]{1,0:T(8,128)S(1)} %bitcast.87, f32[1024,256]{1,0:T(8,128)S(1)} %bitcast.99), kind=kOutput, calls=%fused_computation.131 | convolution fusion | flops 3221225472 | bytes 11534336 | tf_op jit(solution)/shard_map/dot_general | solution.py:123
  79.0 1.9 fusion.47
  82.0 3.0 %convolution_add_fusion.6 = f32[256,1024]{0,1:T(8,128)} fusion(f32[256,1024]{0,1:T(8,128)S(1)} %fusion.47, f32[1024,1024]{1,0:T(8,128)S(1)} %copy-done.4, f32[2048,256]{1,0:T(8,128)S(1)} %fusion.107, f32[2048,256]{1,0:T(8,128)S(1)} %fusion.106), kind=kOutput, calls=%fused_computation.14 | convolution fusion | flops 1611661312 | bytes 10485760 | tf_op jit(solution)/shard_map/dot_general | solution.py:128
  84.9 5.3 %all-to-all-start.1 = ((f32[8,128,256]{2,1,0:T(8,128)}), f32[8,128,256]{2,1,0:T(8,128)}, u32[]{:S(2)}, u32[]{:S(2)}) async-start(f32[8,128,256]{2,1,0:T(8,128)} %bitcast.12), calls=%async_computation.1 | async-start | bytes 2097152 | tf_op jit(solution)/shard_map/all_to_all | solution.py:164
  92.3 1.2 slice.124
  95.2 2.3 fusion
  99.1 2.3 multiply_reduce_fusion.2
  101.4 6.2 %psum.14 = f32[128]{0:T(128)S(1)} all-reduce(f32[128]{0:T(128)S(1)} %get-tuple-element.12), channel_id=1, replica_groups=mesh['ctx'=8,'chan'=4] {'chan'}, use_global_device_ids=true, to_apply=%region_1.0 | all-reduce | flops 128 | bytes 1024 | tf_op jit(solution)/shard_map/psum | solution.py:219
  108.1 7.4 %all-to-all-done.1 = f32[8,128,256]{2,1,0:T(8,128)} async-done(((f32[8,128,256]{2,1,0:T(8,128)}), f32[8,128,256]{2,1,0:T(8,128)}, u32[]{:S(2)}, u32[]{:S(2)}) %all-to-all-start.1) | async-done | bytes 1048608 | tf_op jit(solution)/shard_map/all_to_all | solution.py:164
  115.5 1.4 copy.55
  118.2 3.3 %multiply_reduce_fusion = (f32[2048]{0:T(1024)S(1)}, f32[128]{0:T(128)}, f32[128,2048]{1,0:T(8,128)}, f32[128,2048]{1,0:T(8,128)S(1)}) fusion(f32[128,2048]{1,0:T(8,128)S(1)} %copy-done.18, f32[128]{0:T(128)S(1)} %copy-done.35, f32[128,2048]{1,0:T(8,128)S(1)} %bitcast.89, f32[128,2048]{1,0:T(8,128)} %param.23, f32[2048]{0:T(1024)S(1)} %copy-done.33, f32[]{:T(128)} %bitcast.17), kind=kLoop, calls=%fused_computation.38 | loop fusion | flops 3143552 | bytes 5260292 | tf_op jit(solution)/shard_map/reduce_sum | solution.py:229
  122.6 4.2 %all-to-all-start.2 = ((f32[8,128,256]{2,1,0:T(8,128)}), f32[8,128,256]{2,1,0:T(8,128)}, u32[]{:S(2)}, u32[]{:S(2)}) async-start(f32[8,128,256]{2,1,0:T(8,128)} %bitcast.96), calls=%async_computation.2 | async-start | bytes 2097152 | tf_op jit(solution)/shard_map/all_to_all | solution.py:157
  127.5 6.7 %psum.15 = f32[128]{0:T(128)} all-reduce(f32[128]{0:T(128)} %get-tuple-element.9), channel_id=1, replica_groups=mesh['ctx'=8,'chan'=4] {'chan'}, use_global_device_ids=true, to_apply=%region_3.0 | all-reduce | flops 128 | bytes 1024 | tf_op jit(solution)/shard_map/psum | solution.py:231
  134.8 3.7 %fusion.102 = (f32[128,2048]{1,0:T(8,128)}, f32[128,2048]{1,0:T(8,128)S(1)}) fusion(f32[128,2048]{1,0:T(8,128)} %get-tuple-element.22, f32[128]{0:T(128)S(1)} %broadcast_multiply_fusion, f32[128,2048]{1,0:T(8,128)} %get-tuple-element.13, f32[128]{0:T(128)} %get-tuple-element.20, f32[128,2048]{1,0:T(8,128)S(1)} %copy-done.13, f32[128,2048]{1,0:T(8,128)} %bitcast.90, ...), kind=kLoop, calls=%fused_computation.127 | loop fusion | flops 2097152 | bytes 7349760 | tf_op jit(solution)/shard_map/mul | solution.py:235
  141.0 1.7 fusion.1
  142.7 8.3 %all-to-all-done.2 = f32[8,128,256]{2,1,0:T(8,128)} async-done(((f32[8,128,256]{2,1,0:T(8,128)}), f32[8,128,256]{2,1,0:T(8,128)}, u32[]{:S(2)}, u32[]{:S(2)}) %all-to-all-start.2) | async-done | bytes 1048608 | tf_op jit(solution)/shard_map/all_to_all | solution.py:157
  151.0 1.2 slice.134
  152.9 1.4 maximum_add_fusion
  155.3 4.5 %all-to-all-start.3 = ((f32[8,136,256]{2,1,0:T(8,128)}), f32[8,136,256]{2,1,0:T(8,128)}, u32[]{:S(2)}, u32[]{:S(2)}) async-start(f32[8,136,256]{2,1,0:T(8,128)} %bitcast.84), calls=%async_computation.3 | async-start | bytes 2228224 | tf_op jit(solution)/shard_map/all_to_all | solution.py:157
  161.0 6.3 %fusion.20 = f32[2048,256]{1,0:T(8,128)S(1)} fusion(f32[2048,1024]{1,0:T(8,128)} %constant.26.clone, f32[1024,256]{1,0:T(8,128)} %bitcast.21, f32[]{:T(128)} %bitcast.27), kind=kOutput, calls=%fused_computation.34 | convolution fusion | flops 3221487616 | bytes 11534340 | tf_op jit(solution)/shard_map/dot_general | solution.py:123
  167.4 3.0 %fusion.16 = f32[256,1024]{0,1:T(8,128)} fusion(f32[1024,1024]{1,0:T(8,128)S(1)} %copy-done.3, f32[2048,256]{1,0:T(8,128)S(1)} %fusion.20, f32[2048,256]{1,0:T(8,128)S(1)} %copy-done.8), kind=kOutput, calls=%fused_computation.30 | convolution fusion | flops 1611399168 | bytes 9437184 | tf_op jit(solution)/shard_map/dot_general | solution.py:128
  170.3 15.4 %all-to-all-done.3 = f32[8,136,256]{2,1,0:T(8,128)} async-done(((f32[8,136,256]{2,1,0:T(8,128)}), f32[8,136,256]{2,1,0:T(8,128)}, u32[]{:S(2)}, u32[]{:S(2)}) %all-to-all-start.3) | async-done | bytes 1114144 | tf_op jit(solution)/shard_map/all_to_all | solution.py:157
  185.7 1.2 slice.140
  187.5 5.9 %fusion.5 = f32[256,1024]{0,1:T(8,128)} fusion(f32[256,1024]{0,1:T(8,128)} %fusion.16, f32[1024,1024]{1,0:T(8,128)} %constant.32, f32[2048,256]{1,0:T(8,128)S(1)} %fusion.20, f32[2048,256]{1,0:T(8,128)} %copy-done.7, f32[]{:T(128)} %bitcast.29), kind=kOutput, calls=%fused_computation.13 | convolution fusion | flops 1611923456 | bytes 10485764 | tf_op jit(solution)/shard_map/dot_general | solution.py:128
  193.5 4.2 %all-to-all-start.4 = ((f32[8,128,256]{2,1,0:T(8,128)}), f32[8,128,256]{2,1,0:T(8,128)}, u32[]{:S(2)}, u32[]{:S(2)}) async-start(f32[8,128,256]{2,1,0:T(8,128)} %bitcast.95), calls=%async_computation.4 | async-start | bytes 2097152 | tf_op jit(solution)/shard_map/all_to_all | solution.py:164
  197.8 1.3 collective-permute-start.1
  199.1 5.7 %fusion.9 = f32[256,1024]{0,1:T(8,128)} fusion(f32[1024,1024]{1,0:T(8,128)} %constant.31, f32[2048,256]{1,0:T(8,128)S(1)} %fusion.20, f32[2048,256]{1,0:T(8,128)} %copy-done.5), kind=kOutput, calls=%fused_computation.23 | convolution fusion | flops 1611399168 | bytes 9437184 | tf_op jit(solution)/shard_map/dot_general | solution.py:128
  204.7 2.0 reduce_sum.39
  206.7 19.7 %all-to-all-done.4 = f32[8,128,256]{2,1,0:T(8,128)} async-done(((f32[8,128,256]{2,1,0:T(8,128)}), f32[8,128,256]{2,1,0:T(8,128)}, u32[]{:S(2)}, u32[]{:S(2)}) %all-to-all-start.4) | async-done | bytes 1048608 | tf_op jit(solution)/shard_map/all_to_all | solution.py:164
  226.4 1.5 copy.56
  230.1 5.4 %fusion.4 = f32[256,1024]{0,1:T(8,128)} fusion(f32[256,1024]{0,1:T(8,128)} %fusion.9, f32[1024,1024]{1,0:T(8,128)} %constant.32, f32[2048,256]{1,0:T(8,128)S(1)} %fusion.20, f32[2048,256]{1,0:T(8,128)S(1)} %copy-done.6, f32[]{:T(128)} %bitcast.33), kind=kOutput, calls=%fused_computation.11 | convolution fusion | flops 1611923456 | bytes 10485764 | tf_op jit(solution)/shard_map/dot_general | solution.py:128
  235.5 4.6 %all-to-all-start.5 = ((f32[8,128,256]{2,1,0:T(8,128)}), f32[8,128,256]{2,1,0:T(8,128)}, u32[]{:S(2)}, u32[]{:S(2)}) async-start(f32[8,128,256]{2,1,0:T(8,128)} %bitcast.92), calls=%async_computation.5 | async-start | bytes 2097152 | tf_op jit(solution)/shard_map/all_to_all | solution.py:164
  240.2 2.4 convolution_add_fusion
  244.5 2.2 fusion.104
  246.7 1.1 mul.253
  247.8 16.1 %all-gather.2.cloned.1.call-done = f32[136,2048]{1,0:T(8,128)} async-done(((f32[136,256]{1,0:T(8,128)}), f32[136,2048]{1,0:T(8,128)}) %all-gather.2.cloned.1.call-update) | async-done | bytes 1114128 | tf_op jit(solution)/shard_map/all_gather | solution.py:253
  263.9 2.3 slice.135
  266.2 1.4 slice.136
  267.7 14.7 %all-to-all-done.5 = f32[8,128,256]{2,1,0:T(8,128)} async-done(((f32[8,128,256]{2,1,0:T(8,128)}), f32[8,128,256]{2,1,0:T(8,128)}, u32[]{:S(2)}, u32[]{:S(2)}) %all-to-all-start.5) | async-done | bytes 1048608 | tf_op jit(solution)/shard_map/all_to_all | solution.py:164
  282.3 2.3 copy.57
  (98 shorter events, 16.9 us)
Async XLA Ops:
  7.2 84.1 %copy-start = (f32[128,2048]{1,0:T(8,128)S(1)}, f32[128,2048]{1,0:T(8,128)}, u32[]{:S(2)}) copy-start(f32[128,2048]{1,0:T(8,128)} %param.24) | copy-start | bytes 3145732
  7.2 1.9 copy-start.28
  10.9 7.4 %copy-start.19 = (f32[128,2048]{1,0:T(8,128)S(1)}, f32[128,2048]{1,0:T(8,128)}, u32[]{:S(2)}) copy-start(f32[128,2048]{1,0:T(8,128)} %param.19) | copy-start | bytes 3145732
  10.9 55.8 %all-to-all-start = ((f32[8,256,256]{2,1,0:T(8,128)}), f32[8,256,256]{2,1,0:T(8,128)}, u32[]{:S(2)}, u32[]{:S(2)}) async-start(f32[8,256,256]{2,1,0:T(8,128)} %pad_maximum_fusion), calls=%async_computation | async-start | bytes 4194304 | tf_op jit(solution)/shard_map/all_to_all | solution.py:174
  19.6 74.6 %collective-permute-start = (f32[128,2048]{1,0:T(8,128)S(1)}, f32[128,2048]{1,0:T(8,128)S(1)}, u32[]{:S(2)}, u32[]{:S(2)}) collective-permute-start(f32[128,2048]{1,0:T(8,128)S(1)} %mul.200), channel_id=1, source_target_pairs={{0,4},{4,8},{8,12},{12,16},{16,20},{20,24},{24,28},{1,5},{5,9},{9,... | collective-permute-start | bytes 3145736 | tf_op jit(solution)/shard_map/ppermute | solution.py:14
  66.7 8.6 %slice-start = ((s8[8388608]{0:T(1024)(128)(4,1)}), s8[4194304]{0:T(1024)(128)(4,1)S(1)}, s32[]{:S(2)}) async-start(s8[8388608]{0:T(1024)(128)(4,1)} %bitcast.86), calls=%async_computation.7 | async-start | bytes 8388608
  68.5 6.7 %slice-start.1 = ((s8[8388608]{0:T(1024)(128)(4,1)}), s8[4194304]{0:T(1024)(128)(4,1)S(1)}, s32[]{:S(2)}) async-start(s8[8388608]{0:T(1024)(128)(4,1)} %bitcast.86), calls=%async_computation.8 | async-start | bytes 8388608
  75.2 5.7 %copy-start.5 = (f32[2048,256]{1,0:T(8,128)}, f32[2048,256]{1,0:T(8,128)S(1)}, u32[]{:S(2)}) copy-start(f32[2048,256]{1,0:T(8,128)S(1)} %fusion.107) | copy-start | bytes 6291460
  75.3 3.7 %copy-start.2 = (f32[1024,1024]{1,0:T(8,128)S(1)}, f32[1024,1024]{1,0:T(8,128)}, u32[]{:S(2)}) copy-start(f32[1024,1024]{1,0:T(8,128)} %constant.31) | copy-start | bytes 12582916
  79.0 2.0 copy-start.7
  79.0 2.9 %copy-start.4 = (f32[1024,1024]{1,0:T(8,128)S(1)}, f32[1024,1024]{1,0:T(8,128)}, u32[]{:S(2)}) copy-start(f32[1024,1024]{1,0:T(8,128)} %constant.32) | copy-start | bytes 12582916
  84.9 5.3 %copy-start.27 = (f32[256,128]{1,0:T(8,128)S(1)}, f32[256,128]{1,0:T(8,128)}, u32[]{:S(2)}) copy-start(f32[256,128]{1,0:T(8,128)} %constant.28.clone) | copy-start | bytes 393220
  84.9 30.6 %all-to-all-start.1 = ((f32[8,128,256]{2,1,0:T(8,128)}), f32[8,128,256]{2,1,0:T(8,128)}, u32[]{:S(2)}, u32[]{:S(2)}) async-start(f32[8,128,256]{2,1,0:T(8,128)} %bitcast.12), calls=%async_computation.1 | async-start | bytes 2097152 | tf_op jit(solution)/shard_map/all_to_all | solution.py:164
  91.3 3.9 %copy-start.32 = (f32[256,128]{1,0:T(8,128)S(1)}, f32[256,128]{1,0:T(8,128)}, u32[]{:S(2)}) copy-start(f32[256,128]{1,0:T(8,128)} %constant.29.clone) | copy-start | bytes 393220
  92.3 6.0 %copy-start.11 = (f32[256,2048]{0,1:T(8,128)}, f32[256,2048]{0,1:T(8,128)S(1)}, u32[]{:S(2)}) copy-start(f32[256,2048]{0,1:T(8,128)S(1)} %fusion.108) | copy-start | bytes 6291460
  94.2 1.0 copy-start.29
  95.2 2.3 copy-start.31
  97.5 1.2 copy-start.20
  97.5 1.5 copy-start.24
  97.5 1.5 copy-start.30
  101.4 16.8 %copy-start.33 = (f32[2048]{0:T(1024)S(1)}, f32[2048]{0:T(1024)}, u32[]{:S(2)}) copy-start(f32[2048]{0:T(1024)} %param.26) | copy-start | bytes 24580
  115.5 2.7 copy-start.18
  115.5 2.7 copy-start.35
  117.0 4.5 %copy-start.15 = (f32[8,16,8,256]{3,2,0,1:T(8,128)}, f32[8,16,8,256]{3,2,0,1:T(8,128)S(1)}, u32[]{:S(2)}) copy-start(f32[8,16,8,256]{3,2,0,1:T(8,128)S(1)} %copy.55) | copy-start | bytes 3145732
  121.5 13.3 %copy-start.13 = (f32[128,2048]{1,0:T(8,128)S(1)}, f32[128,2048]{1,0:T(8,128)}, u32[]{:S(2)}) copy-start(f32[128,2048]{1,0:T(8,128)} %param.27) | copy-start | bytes 3145732
  122.6 28.5 %all-to-all-start.2 = ((f32[8,128,256]{2,1,0:T(8,128)}), f32[8,128,256]{2,1,0:T(8,128)}, u32[]{:S(2)}, u32[]{:S(2)}) async-start(f32[8,128,256]{2,1,0:T(8,128)} %bitcast.96), calls=%async_computation.2 | async-start | bytes 2097152 | tf_op jit(solution)/shard_map/all_to_all | solution.py:157
  134.8 3.7 %copy-start.25 = (f32[128,2048]{1,0:T(8,128)S(1)}, f32[128,2048]{1,0:T(8,128)}, u32[]{:S(2)}) copy-start(f32[128,2048]{1,0:T(8,128)} %param.20) | copy-start | bytes 3145732
  138.5 1.2 copy-start.16
  139.6 1.4 copy-start.9
  141.0 11.9 %copy-start.34 = (f32[136]{0:T(256)S(1)}, f32[136]{0:T(256)}, u32[]{:S(2)}) copy-start(f32[136]{0:T(256)} %pad.2.clone) | copy-start | bytes 1636
  155.3 30.4 %all-to-all-start.3 = ((f32[8,136,256]{2,1,0:T(8,128)}), f32[8,136,256]{2,1,0:T(8,128)}, u32[]{:S(2)}, u32[]{:S(2)}) async-start(f32[8,136,256]{2,1,0:T(8,128)} %bitcast.84), calls=%async_computation.3 | async-start | bytes 2228224 | tf_op jit(solution)/shard_map/all_to_all | solution.py:157
  161.0 6.4 %copy-start.3 = (f32[1024,1024]{1,0:T(8,128)S(1)}, f32[1024,1024]{1,0:T(8,128)}, u32[]{:S(2)}) copy-start(f32[1024,1024]{1,0:T(8,128)} %constant.31) | copy-start | bytes 12582916
  161.0 6.4 %copy-start.8 = (f32[2048,256]{1,0:T(8,128)S(1)}, f32[2048,256]{1,0:T(8,128)}, u32[]{:S(2)}) copy-start(f32[2048,256]{1,0:T(8,128)} %copy-done.7) | copy-start | bytes 6291460
  193.5 33.0 %all-to-all-start.4 = ((f32[8,128,256]{2,1,0:T(8,128)}), f32[8,128,256]{2,1,0:T(8,128)}, u32[]{:S(2)}, u32[]{:S(2)}) async-start(f32[8,128,256]{2,1,0:T(8,128)} %bitcast.95), calls=%async_computation.4 | async-start | bytes 2097152 | tf_op jit(solution)/shard_map/all_to_all | solution.py:164
  197.7 66.2 %all-gather.2.cloned.1.call-start = ((), (), s32[]{:S(2)}) async-start(), calls=%async_computation.6 | async-start | bytes 1253376 | tf_op jit(solution)/shard_map/all_gather | solution.py:253
  197.8 42.4 %collective-permute-start.1 = (f32[128,2048]{1,0:T(8,128)S(1)}, f32[128,2048]{1,0:T(8,128)}, u32[]{:S(2)}, u32[]{:S(2)}) collective-permute-start(f32[128,2048]{1,0:T(8,128)S(1)} %mul.224), channel_id=1, source_target_pairs={{4,0},{8,4},{12,8},{16,12},{20,16},{24,20},{28,24},{5,1},{9,5},{13... | collective-permute-start | bytes 3145736 | tf_op jit(solution)/shard_map/ppermute | solution.py:14
  226.4 3.6 %copy-start.6 = (f32[2048,256]{1,0:T(8,128)S(1)}, f32[2048,256]{1,0:T(8,128)}, u32[]{:S(2)}) copy-start(f32[2048,256]{1,0:T(8,128)} %copy-done.5) | copy-start | bytes 6291460
  227.9 1.0 copy-start.22
  235.5 4.7 %copy-start.10 = (f32[256,2048]{0,1:T(8,128)S(1)}, f32[256,2048]{0,1:T(8,128)}, u32[]{:S(2)}) copy-start(f32[256,2048]{0,1:T(8,128)} %copy-done.9) | copy-start | bytes 6291460
  235.5 46.8 %all-to-all-start.5 = ((f32[8,128,256]{2,1,0:T(8,128)}), f32[8,128,256]{2,1,0:T(8,128)}, u32[]{:S(2)}, u32[]{:S(2)}) async-start(f32[8,128,256]{2,1,0:T(8,128)} %bitcast.92), calls=%async_computation.5 | async-start | bytes 2097152 | tf_op jit(solution)/shard_map/all_to_all | solution.py:164
  240.2 2.5 copy-start.12
  242.6 1.2 copy-start.17
  242.6 1.5 copy-start.21
  242.7 1.9 copy-start.26
  244.5 2.2 copy-start.14
  244.5 2.2 copy-start.23
  246.7 37.9 %copy-start.1 = (f32[128,2048]{1,0:T(8,128)S(1)}, f32[128,2048]{1,0:T(8,128)}, u32[]{:S(2)}) copy-start(f32[128,2048]{1,0:T(8,128)} %param.24) | copy-start | bytes 3145732
Sparse Core Ops, SparseCore 0:
  206.9 57.0 all-gather.1
